TPU v7x, 512 devices: a whole 4x4x16 slice. The times are simulated.
512 devices in a mesh: gx: 16 (over z), gy: 16 (over y, x), gz: 2 (over core).
Axes of the slice: x: 4, y: 4, z: 16, core: 2. Of those that a mesh axis runs over, the one named last changes fastest.
Arguments:
- fields: float32 [4, 16, 768, 2048], P(None, 'gz', 'gx', 'gy'), may hold values from -6 to 6
Outputs:
- details_one: float32 [7, 4, 8, 384, 1024], P(None, 'gz', None, 'gx', 'gy')
- details_two: float32 [7, 4, 4, 192, 512], P(None, 'gz', None, 'gx', 'gy')
- details_three: float32 [7, 4, 2, 96, 256], P(None, 'gz', None, 'gx', 'gy')
- details_four: float32 [7, 4, 1, 48, 128], P(None, 'gz', None, 'gx', 'gy')
- coarsest: float32 [4, 1, 48, 128], P('gz', None, 'gx', 'gy')
All inputs are finite; a program needn't handle non-finite values.
Results may differ from a plain program's by a relative error of at most 0.000027.
Values sent between devices are 32-bit elements; how exact they have to be, the bound alone decides.
A program may use at most 64 MiB of HBM per device.

v0:
```python
import functools

import jax
import jax.numpy as jnp
import numpy as np
from jax import lax
from jax.experimental import pallas as pl
from jax.experimental.pallas import tpu as pltpu
from jax.sharding import PartitionSpec as P

MESH = pl.DeviceIdType.MESH
LEVELS = 4
NX, NY, NZ = 48, 128, 8

lift_alpha = -1.586134342059924
lift_beta = -0.052980118572961
lift_gamma = 0.882911075530934
lift_delta = 0.443506852043971
scale_low = 0.869864451624781
scale_high = 1.149604398860241


def lift_halves(even, odd, up, down):
    one = odd + lift_alpha * (even + up(even))
    two = even + lift_beta * (down(one) + one)
    three = one + lift_gamma * (two + up(two))
    four = two + lift_delta * (down(three) + three)
    return four * scale_low, three * scale_high


def operators(extent):
    tiles = 9
    line = np.zeros((tiles * extent, extent))
    line[4 * extent : 5 * extent] = np.eye(extent)
    found = []
    for level in range(LEVELS):
        low, high = lift_halves(
            line[0::2], line[1::2], lambda a: np.roll(a, -1, 0), lambda a: np.roll(a, 1, 0)
        )
        count = extent >> (level + 1)
        start = 4 * count
        pair = []
        for band in (low, high):
            rows = {}
            for k in range(band.shape[0]):
                if np.any(band[k]):
                    rows[k - start] = band[k]
            pair.append(rows)
        found.append(pair)
        line = low
    return found


ROWS_X = operators(NX)
ROWS_Y = operators(NY)
PAD_X = (24, 16, 8, 8)
PLANES = (32, 16, 8, 4)


def split_rows(pair, count):
    groups = {"own": [], "left": [], "right": [], "far": []}
    for band, rows in enumerate(pair):
        for k in sorted(rows):
            if k < -count or k >= 2 * count + 1:
                raise ValueError
            name = "left" if k < 0 else "own" if k < count else "right" if k < 2 * count else "far"
            groups[name].append((band, k, rows[k]))
    return groups


GX = [split_rows(ROWS_X[i], NX >> (i + 1)) for i in range(LEVELS)]
GY = [split_rows(ROWS_Y[i], NY >> (i + 1)) for i in range(LEVELS)]


def x_own(level):
    m = np.zeros((2 * PAD_X[level], NX), np.float32)
    for band, k, w in GX[level]["own"]:
        m[band * PAD_X[level] + k] = w
    return m


def x_edge(level):
    if level == 0:
        m = np.zeros((16, 2 * NX), np.float32)
        for side, name in enumerate(("left", "right")):
            for i, (_, _, w) in enumerate(GX[0][name]):
                for v in range(2):
                    m[8 * side + 4 * v + i, v * NX : (v + 1) * NX] = w
        return m
    m = np.zeros((16, NX), np.float32)
    for side, name in enumerate(("left", "right")):
        rows = list(GX[level][name])
        if side:
            rows = rows + GX[level]["far"]
        for i, (_, _, w) in enumerate(rows):
            m[8 * side + i] = w
    return m


def y_own(level):
    m = np.zeros((NY, 128), np.float32)
    for band, k, w in GY[level]["own"]:
        m[:, band * 64 + k] = w
    return m


def y_edge(level):
    m = np.zeros((16, NY), np.float32)
    for side, name in enumerate(("left", "right")):
        for i, (_, _, w) in enumerate(GY[level][name]):
            m[8 * side + i] = w
    return m


def y_place(level):
    count = NY >> (level + 1)
    m = np.zeros((16, 128), np.float32)
    for side, name in enumerate(("left", "right")):
        for i, (band, k, _) in enumerate(GY[level][name]):
            m[8 * side + i, band * 64 + (k + count if side == 0 else k - count)] = 1
    return m


assert not any(GY[i]["far"] for i in range(LEVELS))

def packed_table():
    parts, where, at = [], {}, 0
    for level in range(LEVELS):
        for name, m in (
            ("x_own", x_own(level)),
            ("x_edge", x_edge(level)),
            ("y_own", y_own(level)),
            ("y_edge", y_edge(level)),
            ("y_place", y_place(level)),
        ):
            wide = np.zeros((m.shape[0], 128), np.float32)
            wide[:, : m.shape[1]] = m
            parts.append(wide)
            where[name, level] = (at, m.shape)
            at += m.shape[0]
    return np.concatenate(parts), where


TABLE, WHERE = packed_table()

EDGE_AT = (0, 128, 256, 320)
EDGE_ROWS = (128, 128, 64, 32)
OWN_AT = (0, 1536, 2048, 2176)
OWN_ROWS = tuple(2 * PLANES[i] * PAD_X[i] for i in range(LEVELS))


def exact(a, b):
    return jnp.dot(a, b, precision=lax.Precision.HIGHEST, preferred_element_type=jnp.float32)


def exact_nt(a, b):
    return lax.dot_general(
        a, b, (((1,), (1,)), ((), ())), precision=lax.Precision.HIGHEST, preferred_element_type=jnp.float32
    )


def exact_tn(a, b):
    return lax.dot_general(
        a, b, (((0,), (0,)), ((), ())), precision=lax.Precision.HIGHEST, preferred_element_type=jnp.float32
    )


def stacked(wide, planes):
    return jnp.concatenate([wide[:, 128 * p : 128 * (p + 1)] for p in range(planes)], axis=0)


def kernel(ring_x, ring_y, *refs):
    fields, table_in = refs[:2]
    values = refs[2:6]
    (table, raw, wide1, wide2, wide3, wide4, m_out, c_out, k_out,
     m_in, c_in, k_in, far_m, far_k, send, recv, local) = refs[6:]
    wides = (wide1, wide2, wide3, wide4)

    def op(name, level):
        first, (rows, columns) = WHERE[name, level]
        return table[first : first + rows, :columns]

    gx, gy, gz = lax.axis_index("gx"), lax.axis_index("gy"), lax.axis_index("gz")

    def at(dx, dy):
        return (lax.rem(gx + dx + ring_x, ring_x), lax.rem(gy + dy + ring_y, ring_y), gz)

    partner = (gx, gy, 1 - gz)
    near = [(dx, dy) for dx in (-1, 0, 1) for dy in (-1, 0, 1) if dx or dy]
    barrier = pltpu.get_barrier_semaphore()
    for d in near + [(-2, -1), (-2, 0), (-2, 1)]:
        pl.semaphore_signal(barrier, inc=1, device_id=at(*d), device_id_type=MESH)
    pl.semaphore_signal(barrier, inc=1, device_id=partner, device_id_type=MESH)
    keep = pltpu.make_async_copy(fields.at[pl.ds(2 * gz, 2)], raw.at[:, pl.ds(NZ * gz, NZ)], local.at[0])
    keep.start()
    fill = pltpu.make_async_copy(table_in, table, local.at[1])
    fill.start()
    pl.semaphore_wait(barrier, 12)

    def copy(src, dst, slot, device):
        c = pltpu.make_async_remote_copy(
            src_ref=src, dst_ref=dst, send_sem=send.at[slot], recv_sem=recv.at[slot],
            device_id=device, device_id_type=MESH,
        )
        c.start()
        return c

    swap = copy(fields.at[pl.ds(2 - 2 * gz, 2)], raw.at[:, pl.ds(NZ * gz, NZ)], 0, partner)
    keep.wait()
    fill.wait()
    swap.wait()

    for v in range(2):
        planes = [raw[v, i] for i in range(2 * NZ)]
        for level in range(LEVELS):
            half = len(planes) // 2
            even, odd = planes[0::2], planes[1::2]
            one = [odd[k] + lift_alpha * (even[k] + even[(k + 1) % half]) for k in range(half)]
            two = [even[k] + lift_beta * (one[k - 1] + one[k]) for k in range(half)]
            three = [one[k] + lift_gamma * (two[k] + two[(k + 1) % half]) for k in range(half)]
            four = [two[k] + lift_delta * (three[k - 1] + three[k]) for k in range(half)]
            low = [a * scale_low for a in four]
            high = [a * scale_high for a in three]
            for i, plane in enumerate(low + high):
                if level == 0:
                    wide1[NX * v : NX * (v + 1), 128 * i : 128 * (i + 1)] = plane
                else:
                    j = v * 2 * half + i
                    wides[level][:, 128 * j : 128 * (j + 1)] = plane
            planes = low

    copies = []
    for level in range(LEVELS):
        edge = exact(op("x_edge", level), wides[level][...])
        lanes = 16 if level == 0 else PLANES[level]
        first, count = EDGE_AT[level], EDGE_ROWS[level]
        for side in range(2):
            rows = stacked(edge[8 * side : 8 * side + 8], lanes)
            m_out[side, first : first + count, :] = exact(rows, op("y_own", level))
            corner = exact_nt(op("y_edge", level), rows)
            k_out[side, :, :, first : first + count] = corner.reshape(2, 8, count)
    for side, dx in ((0, -1), (1, 1)):
        copies.append(copy(m_out.at[side], m_in.at[side], 1 + side, at(dx, 0)))
        for up, dy in ((0, -1), (1, 1)):
            copies.append(copy(k_out.at[side, up], k_in.at[side, up], 3 + 2 * side + up, at(dx, dy)))
    copies.append(copy(m_out.at[1, pl.ds(320, 32)], far_m, 7, at(2, 0)))
    for up, dy in ((0, -1), (1, 1)):
        copies.append(copy(k_out.at[1, up, :, pl.ds(256, 128)], far_k.at[up], 8 + up, at(2, dy)))

    tall = []
    for level in range(LEVELS):
        pad, p = PAD_X[level], PLANES[level]
        if level == 0:
            pieces = [exact(op("x_own", 0), wide1[NX * v : NX * (v + 1), :]) for v in range(2)]
            both = jnp.concatenate(pieces, axis=1)
        else:
            both = exact(op("x_own", level), wides[level][...])
        rows = jnp.concatenate([stacked(both[:pad], p), stacked(both[pad:], p)], axis=0)
        first, count = OWN_AT[level], OWN_ROWS[level]
        c_out[:, :, first : first + count] = exact_nt(op("y_edge", level), rows).reshape(2, 8, count)
        tall.append(rows)
    for up, dy in ((0, -1), (1, 1)):
        copies.append(copy(c_out.at[up], c_in.at[up], 10 + up, at(0, dy)))
    for level in range(LEVELS):
        pad, p = PAD_X[level], PLANES[level]
        values[level][...] = exact(tall[level], op("y_own", level)).reshape(2, p, pad, 128)

    for c in copies:
        c.wait()

    row = lax.broadcasted_iota(jnp.int32, (1, 8, 128), 1)

    def shifted(block, start, count, to):
        turn = (to - start) % 8
        if turn:
            block = pltpu.roll(block, turn, 1)
        return jnp.where((row >= to) & (row < to + count), block, 0.0)

    for level in range(LEVELS):
        pad, p = PAD_X[level], PLANES[level]
        count_x = NX >> (level + 1)
        first, count = OWN_AT[level], OWN_ROWS[level]
        c = c_in[:, :, first : first + count].reshape(16, count)
        values[level][...] += exact_tn(c, op("y_place", level)).reshape(2, p, pad, 128)
        first, count = EDGE_AT[level], EDGE_ROWS[level]
        for side in range(2):
            k = k_in[side, :, :, first : first + count].reshape(16, count)
            m = m_in[side, first : first + count, :] + exact_tn(k, op("y_place", level))
            if level == 3 and side == 1:
                k = far_k[:, :, 64:96].reshape(16, count)
                far = far_m[...] + exact_tn(k, op("y_place", level))
            block = m.reshape(count // 8, 8, 128)
            edges = GX[level]["right" if side else "left"]
            for bx in range(2):
                hits = [i for i, h in enumerate(edges) if h[0] == bx]
                k0 = edges[hits[0]][1]
                to = k0 - count_x if side else k0 + count_x
                base = to - to % 8
                if level == 0:
                    for v in range(2):
                        add = shifted(block, hits[0] + 4 * v, len(hits), to - base)
                        values[0][bx, 16 * v : 16 * v + 16, base : base + 8, :] += add
                else:
                    add = shifted(block, hits[0], len(hits), to - base)
                    if level == 3 and side == 1 and bx == 0:
                        add = add + shifted(far.reshape(count // 8, 8, 128), 6, 1, 0)
                    values[level][bx, :, base : base + 8, :] += add


def finish(*refs):
    values, outs, stages, sems = refs[:4], refs[4:9], refs[9:14], refs[14]
    copies = []
    for level in range(LEVELS):
        half = 8 >> level
        rows, columns = NX >> (level + 1), NY >> (level + 1)
        for bx in range(2):
            for by in range(2):
                for bz in range(2):
                    b = 4 * bz + 2 * by + bx
                    if b == 0 and level < 3:
                        continue
                    for v in range(2):
                        j = (2 * v + bz) * half
                        got = values[level][bx, j : j + half, :rows, 64 * by : 64 * by + columns]
                        if level == 0:
                            stages[0][b - 1, v] = got
                        else:
                            for z in range(half):
                                if b == 0:
                                    stages[4][v * rows : (v + 1) * rows, z, :] = got[z]
                                else:
                                    stages[level][b - 1, v, :, z, :] = got[z]
        copies.append(pltpu.make_async_copy(stages[level], outs[level], sems.at[level]))
        copies[-1].start()
    copies.append(pltpu.make_async_copy(stages[4], outs[4], sems.at[4]))
    copies[-1].start()
    for c in copies:
        c.wait()


def in_hbm(array):
    return pltpu.with_memory_space_constraint(array, pltpu.HBM)


def solution(mesh):
    ring_x, ring_y = mesh.shape["gx"], mesh.shape["gy"]
    shapes = [(7, 2, 8, NX >> 1, NY >> 1)]
    shapes += [(7, 2, NX >> (i + 1), 8 >> i, NY >> (i + 1)) for i in range(1, LEVELS)]
    shapes.append((2 * (NX >> LEVELS), 1, NY >> LEVELS))
    f32 = jnp.float32
    any_ = pl.BlockSpec(memory_space=pl.ANY)
    vmem = pl.BlockSpec(memory_space=pltpu.VMEM)

    def body(fields):
        values = pl.pallas_call(
            functools.partial(kernel, ring_x, ring_y),
            out_shape=[pltpu.VMEM((2, PLANES[i], PAD_X[i], 128), f32) for i in range(LEVELS)],
            in_specs=[any_] * 2,
            out_specs=[vmem] * 4,
            scratch_shapes=[
                pltpu.VMEM(TABLE.shape, f32),
                pltpu.VMEM((2, 2 * NZ, NX, NY), f32),
                pltpu.VMEM((2 * NX, 16 * NY), f32),
                pltpu.VMEM((NX, 16 * NY), f32),
                pltpu.VMEM((NX, 8 * NY), f32),
                pltpu.VMEM((NX, 4 * NY), f32),
            ]
            + [pltpu.VMEM((2, 352, 128), f32), pltpu.VMEM((2, 8, 2304), f32), pltpu.VMEM((2, 2, 8, 384), f32)] * 2
            + [
                pltpu.VMEM((32, 128), f32),
                pltpu.VMEM((2, 8, 128), f32),
                pltpu.SemaphoreType.DMA((12,)),
                pltpu.SemaphoreType.DMA((12,)),
                pltpu.SemaphoreType.DMA((2,)),
            ],
            compiler_params=pltpu.CompilerParams(
                collective_id=0, has_side_effects=True, vmem_limit_bytes=40 << 20
            ),
        )(in_hbm(fields), in_hbm(jnp.asarray(TABLE)))
        outs = pl.pallas_call(
            finish,
            out_shape=[pltpu.HBM(s, f32) for s in shapes],
            in_specs=[vmem] * 4,
            out_specs=[any_] * 5,
            scratch_shapes=[pltpu.VMEM(s, f32) for s in shapes] + [pltpu.SemaphoreType.DMA((5,))],
            compiler_params=pltpu.CompilerParams(vmem_limit_bytes=24 << 20),
        )(*values)
        small = [jnp.swapaxes(o, 2, 3) for o in outs[1:4]]
        return (outs[0], *small, outs[4].reshape(2, 1, NX >> LEVELS, NY >> LEVELS))

    in_specs = (P(None, "gz", "gx", "gy"),)
    out_specs = tuple([P(None, "gz", None, "gx", "gy")] * 4 + [P("gz", None, "gx", "gy")])
    return jax.shard_map(body, mesh=mesh, in_specs=in_specs, out_specs=out_specs, check_vma=False)
```

profile of v0, /device:TPU:1, one launch (start us, length us, event | category | flops | bytes accessed | tf_op | source)
XLA Modules:
  0.0 31.7 jit_solution(11965264377659900559)
XLA Ops:
  0.6 29.0 %shard_map.65 = (f32[2,32,24,128]{3,2,1,0:T(8,128)S(1)}, f32[2,16,16,128]{3,2,1,0:T(8,128)S(1)}, f32[2,8,8,128]{3,2,1,0:T(8,128)S(1)}, f32[2,4,8,128]{3,2,1,0:T(8,128)S(1)}) custom-call(f32[4,8,48,128]{3,2,1,0:T(8,128)} %refs_0_.1, f32[816,128]{1,0:T(8,128)} %constant.2.clone.refs_1_), custom_call_target="tpu_custom_call" | custom-call | tf_op jit(solution)/shard_map/pallas_call | solution.py:355
  29.6 2.0 %shard_map.66 = (f32[7,2,8,24,64]{4,3,2,1,0:T(8,128)}, f32[7,2,12,4,32]{4,3,2,1,0:T(4,128)}, f32[7,2,6,2,16]{4,3,2,1,0:T(2,128)}, f32[7,2,3,1,8]{4,3,2,1,0:T(1,128)}, f32[6,1,8]{2,1,0:T(1,128)}) custom-call(f32[2,32,24,128]{3,2,1,0:T(8,128)S(1)} %get-tuple-element.14.refs_0_, f32[2,16,16,128]{3,2,1,0:T(8,128)S(1)} %get-tuple-element.15.refs_1_, ...), custom_call_target="tpu_custom_call" | custom-call | tf_op jit(solution)/shard_map/pallas_call | solution.py:380
where the time goes:
time: 31.8 us; the launch traced here: 31.7 us
  Pallas kernels  31 us (97%)
  between operations  0.64 us (2%)
    pallas_call x1, Pallas kernels, body(): pl.pallas_call(functools.partial(kernel, ring_x, ring_y), out_shape=[pltp...  29 us
    pallas_call x1, Pallas kernels, body(): pl.pallas_call(finish, out_shape=[pltpu.HBM(s, f32) for s in shapes], in_...  2.05 us

commit v1 on v0

--- a/solution.py
+++ b/solution.py
@@ -100,7 +100,7 @@
 def y_own(level):
     m = np.zeros((NY, 128), np.float32)
     for band, k, w in GY[level]["own"]:
-        m[:, band * 64 + k] = w
+        m[:, band * (NY >> (level + 1)) + k] = w
     return m
 
 
@@ -117,7 +117,7 @@
     m = np.zeros((16, 128), np.float32)
     for side, name in enumerate(("left", "right")):
         for i, (band, k, _) in enumerate(GY[level][name]):
-            m[8 * side + i, band * 64 + (k + count if side == 0 else k - count)] = 1
+            m[8 * side + i, band * count + (k + count if side == 0 else k - count)] = 1
     return m
 
 
@@ -143,9 +143,12 @@
 
 TABLE, WHERE = packed_table()
 
-EDGE_AT = (0, 128, 256, 320)
-EDGE_ROWS = (128, 128, 64, 32)
-OWN_AT = (0, 1536, 2048, 2176)
+EDGE_AT = (0, 128, 192, 208)
+EDGE_ROWS = (128, 64, 16, 8)
+EDGE_TURN = (128, 64, 32, 16)
+CORNER_AT = (0, 128, 256, 320)
+CORNER_ROWS = (128, 128, 64, 32)
+OWN_AT = (0, 768, 1280, 1408)
 OWN_ROWS = tuple(2 * PLANES[i] * PAD_X[i] for i in range(LEVELS))
 
 
@@ -169,47 +172,24 @@
     return jnp.concatenate([wide[:, 128 * p : 128 * (p + 1)] for p in range(planes)], axis=0)
 
 
-def kernel(ring_x, ring_y, *refs):
-    fields, table_in = refs[:2]
-    values = refs[2:6]
-    (table, raw, wide1, wide2, wide3, wide4, m_out, c_out, k_out,
-     m_in, c_in, k_in, far_m, far_k, send, recv, local) = refs[6:]
+def planes_kernel(fields, table_in, table, wide1, wide2, wide3, wide4, raw, send, recv, local):
     wides = (wide1, wide2, wide3, wide4)
-
-    def op(name, level):
-        first, (rows, columns) = WHERE[name, level]
-        return table[first : first + rows, :columns]
-
     gx, gy, gz = lax.axis_index("gx"), lax.axis_index("gy"), lax.axis_index("gz")
-
-    def at(dx, dy):
-        return (lax.rem(gx + dx + ring_x, ring_x), lax.rem(gy + dy + ring_y, ring_y), gz)
-
     partner = (gx, gy, 1 - gz)
-    near = [(dx, dy) for dx in (-1, 0, 1) for dy in (-1, 0, 1) if dx or dy]
     barrier = pltpu.get_barrier_semaphore()
-    for d in near + [(-2, -1), (-2, 0), (-2, 1)]:
-        pl.semaphore_signal(barrier, inc=1, device_id=at(*d), device_id_type=MESH)
     pl.semaphore_signal(barrier, inc=1, device_id=partner, device_id_type=MESH)
     keep = pltpu.make_async_copy(fields.at[pl.ds(2 * gz, 2)], raw.at[:, pl.ds(NZ * gz, NZ)], local.at[0])
     keep.start()
     fill = pltpu.make_async_copy(table_in, table, local.at[1])
     fill.start()
-    pl.semaphore_wait(barrier, 12)
-
-    def copy(src, dst, slot, device):
-        c = pltpu.make_async_remote_copy(
-            src_ref=src, dst_ref=dst, send_sem=send.at[slot], recv_sem=recv.at[slot],
-            device_id=device, device_id_type=MESH,
-        )
-        c.start()
-        return c
-
-    swap = copy(fields.at[pl.ds(2 - 2 * gz, 2)], raw.at[:, pl.ds(NZ * gz, NZ)], 0, partner)
+    pl.semaphore_wait(barrier, 1)
+    swap = pltpu.make_async_remote_copy(
+        src_ref=fields.at[pl.ds(2 - 2 * gz, 2)], dst_ref=raw.at[:, pl.ds(NZ * gz, NZ)],
+        send_sem=send, recv_sem=recv, device_id=partner, device_id_type=MESH,
+    )
+    swap.start()
     keep.wait()
-    fill.wait()
     swap.wait()
-
     for v in range(2):
         planes = [raw[v, i] for i in range(2 * NZ)]
         for level in range(LEVELS):
@@ -228,39 +208,81 @@
                     j = v * 2 * half + i
                     wides[level][:, 128 * j : 128 * (j + 1)] = plane
             planes = low
+    fill.wait()
+
+
+def kernel(ring_x, ring_y, *refs):
+    table = refs[0]
+    wides = refs[1:5]
+    values = refs[5:9]
+    (m_out, c_out, k_out, m_in, c_in, k_in, far_m, far_k, send, recv) = refs[9:]
+
+    def op(name, level):
+        first, (rows, columns) = WHERE[name, level]
+        return table[first : first + rows, :columns]
+
+    gx, gy, gz = lax.axis_index("gx"), lax.axis_index("gy"), lax.axis_index("gz")
+
+    def at(dx, dy):
+        return (lax.rem(gx + dx + ring_x, ring_x), lax.rem(gy + dy + ring_y, ring_y), gz)
+
+    near = [(dx, dy) for dx in (-1, 0, 1) for dy in (-1, 0, 1) if dx or dy]
+    barrier = pltpu.get_barrier_semaphore()
+    for d in near + [(-2, -1), (-2, 0), (-2, 1)]:
+        pl.semaphore_signal(barrier, inc=1, device_id=at(*d), device_id_type=MESH)
+
+    def copy(src, dst, slot, device):
+        c = pltpu.make_async_remote_copy(
+            src_ref=src, dst_ref=dst, send_sem=send.at[slot], recv_sem=recv.at[slot],
+            device_id=device, device_id_type=MESH,
+        )
+        c.start()
+        return c
 
     copies = []
     for level in range(LEVELS):
         edge = exact(op("x_edge", level), wides[level][...])
         lanes = 16 if level == 0 else PLANES[level]
-        first, count = EDGE_AT[level], EDGE_ROWS[level]
+        first, rows = EDGE_AT[level], EDGE_ROWS[level]
+        corner_at, count = CORNER_AT[level], CORNER_ROWS[level]
+        both = jnp.concatenate([stacked(edge[:8], lanes), stacked(edge[8:], lanes)], axis=0)
+        done = exact(both, op("y_own", level))
+        corner = exact_nt(op("y_edge", level), both)
         for side in range(2):
-            rows = stacked(edge[8 * side : 8 * side + 8], lanes)
-            m_out[side, first : first + count, :] = exact(rows, op("y_own", level))
-            corner = exact_nt(op("y_edge", level), rows)
-            k_out[side, :, :, first : first + count] = corner.reshape(2, 8, count)
+            one = done[count * side : count * (side + 1)]
+            packed = one[:rows]
+            for g in range(1, count // rows):
+                packed = packed + pltpu.roll(one[rows * g : rows * (g + 1)], EDGE_TURN[level] * g, 1)
+            m_out[side, first : first + rows, :] = packed
+            k_out[side, :, :, corner_at : corner_at + count] = corner[:, count * side : count * (side + 1)].reshape(2, 8, count)
+    pl.semaphore_wait(barrier, 11)
     for side, dx in ((0, -1), (1, 1)):
-        copies.append(copy(m_out.at[side], m_in.at[side], 1 + side, at(dx, 0)))
         for up, dy in ((0, -1), (1, 1)):
-            copies.append(copy(k_out.at[side, up], k_in.at[side, up], 3 + 2 * side + up, at(dx, dy)))
-    copies.append(copy(m_out.at[1, pl.ds(320, 32)], far_m, 7, at(2, 0)))
+            copies.append(copy(k_out.at[side, up], k_in.at[side, up], 2 + 2 * side + up, at(dx, dy)))
     for up, dy in ((0, -1), (1, 1)):
-        copies.append(copy(k_out.at[1, up, :, pl.ds(256, 128)], far_k.at[up], 8 + up, at(2, dy)))
+        copies.append(copy(k_out.at[1, up, :, pl.ds(256, 128)], far_k.at[up], 6 + up, at(2, dy)))
+    copies.append(copy(m_out.at[1, pl.ds(208, 8)], far_m, 8, at(2, 0)))
+    for side, dx in ((0, -1), (1, 1)):
+        copies.append(copy(m_out.at[side], m_in.at[side], side, at(dx, 0)))
 
     tall = []
     for level in range(LEVELS):
         pad, p = PAD_X[level], PLANES[level]
         if level == 0:
-            pieces = [exact(op("x_own", 0), wide1[NX * v : NX * (v + 1), :]) for v in range(2)]
+            pieces = [exact(op("x_own", 0), wides[0][NX * v : NX * (v + 1), :]) for v in range(2)]
             both = jnp.concatenate(pieces, axis=1)
         else:
             both = exact(op("x_own", level), wides[level][...])
         rows = jnp.concatenate([stacked(both[:pad], p), stacked(both[pad:], p)], axis=0)
         first, count = OWN_AT[level], OWN_ROWS[level]
-        c_out[:, :, first : first + count] = exact_nt(op("y_edge", level), rows).reshape(2, 8, count)
+        c = exact_nt(op("y_edge", level), rows)
+        if level == 0:
+            count = count // 2
+            c = c[:, :count].reshape(2, 8, count) + pltpu.roll(c[:, count:].reshape(2, 8, count), 4, 1)
+        c_out[:, :, first : first + count] = c.reshape(2, 8, count)
         tall.append(rows)
     for up, dy in ((0, -1), (1, 1)):
-        copies.append(copy(c_out.at[up], c_in.at[up], 10 + up, at(0, dy)))
+        copies.append(copy(c_out.at[up], c_in.at[up], 9 + up, at(0, dy)))
     for level in range(LEVELS):
         pad, p = PAD_X[level], PLANES[level]
         values[level][...] = exact(tall[level], op("y_own", level)).reshape(2, p, pad, 128)
@@ -280,15 +302,27 @@
         pad, p = PAD_X[level], PLANES[level]
         count_x = NX >> (level + 1)
         first, count = OWN_AT[level], OWN_ROWS[level]
-        c = c_in[:, :, first : first + count].reshape(16, count)
+        if level == 0:
+            c = c_in[:, :, first : first + count // 2]
+            c = jnp.concatenate([c, pltpu.roll(c, 4, 1)], axis=2).reshape(16, count)
+        else:
+            c = c_in[:, :, first : first + count].reshape(16, count)
         values[level][...] += exact_tn(c, op("y_place", level)).reshape(2, p, pad, 128)
-        first, count = EDGE_AT[level], EDGE_ROWS[level]
+        first, rows = EDGE_AT[level], EDGE_ROWS[level]
+        corner_at, count = CORNER_AT[level], CORNER_ROWS[level]
+
+        def opened(packed):
+            parts = [packed]
+            for g in range(1, count // rows):
+                parts.append(pltpu.roll(packed, 128 - EDGE_TURN[level] * g, 1))
+            return jnp.concatenate(parts, axis=0)
+
         for side in range(2):
-            k = k_in[side, :, :, first : first + count].reshape(16, count)
-            m = m_in[side, first : first + count, :] + exact_tn(k, op("y_place", level))
+            k = k_in[side, :, :, corner_at : corner_at + count].reshape(16, count)
+            m = opened(m_in[side, first : first + rows, :]) + exact_tn(k, op("y_place", level))
             if level == 3 and side == 1:
                 k = far_k[:, :, 64:96].reshape(16, count)
-                far = far_m[...] + exact_tn(k, op("y_place", level))
+                far = opened(far_m[...]) + exact_tn(k, op("y_place", level))
             block = m.reshape(count // 8, 8, 128)
             edges = GX[level]["right" if side else "left"]
             for bx in range(2):
@@ -321,7 +355,7 @@
                         continue
                     for v in range(2):
                         j = (2 * v + bz) * half
-                        got = values[level][bx, j : j + half, :rows, 64 * by : 64 * by + columns]
+                        got = values[level][bx, j : j + half, :rows, columns * by : columns * (by + 1)]
                         if level == 0:
                             stages[0][b - 1, v] = got
                         else:
@@ -348,35 +382,42 @@
     shapes += [(7, 2, NX >> (i + 1), 8 >> i, NY >> (i + 1)) for i in range(1, LEVELS)]
     shapes.append((2 * (NX >> LEVELS), 1, NY >> LEVELS))
     f32 = jnp.float32
+    wide_shapes = [(2 * NX, 16 * NY), (NX, 16 * NY), (NX, 8 * NY), (NX, 4 * NY)]
     any_ = pl.BlockSpec(memory_space=pl.ANY)
     vmem = pl.BlockSpec(memory_space=pltpu.VMEM)
 
     def body(fields):
+        prepared = pl.pallas_call(
+            planes_kernel,
+            out_shape=[pltpu.VMEM(s, f32) for s in [TABLE.shape] + wide_shapes],
+            in_specs=[any_] * 2,
+            out_specs=[vmem] * 5,
+            scratch_shapes=[
+                pltpu.VMEM((2, 2 * NZ, NX, NY), f32),
+                pltpu.SemaphoreType.DMA,
+                pltpu.SemaphoreType.DMA,
+                pltpu.SemaphoreType.DMA((2,)),
+            ],
+            compiler_params=pltpu.CompilerParams(
+                collective_id=1, has_side_effects=True, vmem_limit_bytes=16 << 20
+            ),
+        )(in_hbm(fields), in_hbm(jnp.asarray(TABLE)))
         values = pl.pallas_call(
             functools.partial(kernel, ring_x, ring_y),
             out_shape=[pltpu.VMEM((2, PLANES[i], PAD_X[i], 128), f32) for i in range(LEVELS)],
-            in_specs=[any_] * 2,
+            in_specs=[vmem] * 5,
             out_specs=[vmem] * 4,
-            scratch_shapes=[
-                pltpu.VMEM(TABLE.shape, f32),
-                pltpu.VMEM((2, 2 * NZ, NX, NY), f32),
-                pltpu.VMEM((2 * NX, 16 * NY), f32),
-                pltpu.VMEM((NX, 16 * NY), f32),
-                pltpu.VMEM((NX, 8 * NY), f32),
-                pltpu.VMEM((NX, 4 * NY), f32),
-            ]
-            + [pltpu.VMEM((2, 352, 128), f32), pltpu.VMEM((2, 8, 2304), f32), pltpu.VMEM((2, 2, 8, 384), f32)] * 2
+            scratch_shapes=[pltpu.VMEM((2, 216, 128), f32), pltpu.VMEM((2, 8, 1536), f32), pltpu.VMEM((2, 2, 8, 384), f32)] * 2
             + [
-                pltpu.VMEM((32, 128), f32),
+                pltpu.VMEM((8, 128), f32),
                 pltpu.VMEM((2, 8, 128), f32),
-                pltpu.SemaphoreType.DMA((12,)),
-                pltpu.SemaphoreType.DMA((12,)),
-                pltpu.SemaphoreType.DMA((2,)),
+                pltpu.SemaphoreType.DMA((11,)),
+                pltpu.SemaphoreType.DMA((11,)),
             ],
             compiler_params=pltpu.CompilerParams(
                 collective_id=0, has_side_effects=True, vmem_limit_bytes=40 << 20
             ),
-        )(in_hbm(fields), in_hbm(jnp.asarray(TABLE)))
+        )(*prepared)
         outs = pl.pallas_call(
             finish,
             out_shape=[pltpu.HBM(s, f32) for s in shapes],

time: 31.8 us -> 28.1 us (0.88)
  Pallas kernels: 31 us -> 27.3 us
    pallas_call x1, Pallas kernels: 29 us -> 15.7 us  [body(): pl.pallas_call(functools.partial(kernel, ring_x, ring_y), out_shape=[pltp...]
    pallas_call x0 -> x1, Pallas kernels: none -> 9.55 us  [body(): pl.pallas_call(planes_kernel, out_shape=[pltpu.VMEM(s, f32) for s in [TAB...]
where the time goes in v1:
time: 28.1 us; the launch traced here: 28 us
  Pallas kernels  27.3 us (97%)
  between operations  0.65 us (2%)
    pallas_call x1, Pallas kernels, body(): pl.pallas_call(functools.partial(kernel, ring_x, ring_y), out_shape=[pltp...  15.7 us
    pallas_call x1, Pallas kernels, body(): pl.pallas_call(planes_kernel, out_shape=[pltpu.VMEM(s, f32) for s in [TAB...  9.55 us
    pallas_call x1, Pallas kernels, body(): pl.pallas_call(finish, out_shape=[pltpu.HBM(s, f32) for s in shapes], in_...  2.05 us

profile of v1, /device:TPU:1, one launch (start us, length us, event | category | flops | bytes accessed | tf_op | source)
XLA Modules:
  0.0 28.0 jit_solution(15859699232552959142)
XLA Ops:
  0.6 9.6 %shard_map.65 = (f32[816,128]{1,0:T(8,128)S(1)}, f32[96,2048]{1,0:T(8,128)S(1)}, f32[48,2048]{1,0:T(8,128)S(1)}, f32[48,1024]{1,0:T(8,128)S(1)}, f32[48,512]{1,0:T(8,128)S(1)}) custom-call(f32[4,8,48,128]{3,2,1,0:T(8,128)} %fields.1, f32[816,128]{1,0:T(8,128)} %constant.2.clone.table_in), custom_call_target="tpu_custom_call" | custom-call | tf_op jit(solution)/shard_map/pallas_call | solution.py:390
  10.2 15.7 %shard_map.66 = (f32[2,32,24,128]{3,2,1,0:T(8,128)S(1)}, f32[2,16,16,128]{3,2,1,0:T(8,128)S(1)}, f32[2,8,8,128]{3,2,1,0:T(8,128)S(1)}, f32[2,4,8,128]{3,2,1,0:T(8,128)S(1)}) custom-call(f32[816,128]{1,0:T(8,128)S(1)} %get-tuple-element.19.refs_0_, f32[96,2048]{1,0:T(8,128)S(1)} %get-tuple-element.20.refs_1_, f32[48,2048]{1,0:T(8,128)S(1)} %get-tuple-element.21.refs_2_, ...), custom_call_target="tpu_custom_call" | custom-call | tf_op jit(solution)/shard_map/pallas_call | solution.py:405
  25.9 2.0 %shard_map.67 = (f32[7,2,8,24,64]{4,3,2,1,0:T(8,128)}, f32[7,2,12,4,32]{4,3,2,1,0:T(4,128)}, f32[7,2,6,2,16]{4,3,2,1,0:T(2,128)}, f32[7,2,3,1,8]{4,3,2,1,0:T(1,128)}, f32[6,1,8]{2,1,0:T(1,128)}) custom-call(f32[2,32,24,128]{3,2,1,0:T(8,128)S(1)} %get-tuple-element.24.refs_0_, f32[2,16,16,128]{3,2,1,0:T(8,128)S(1)} %get-tuple-element.25.refs_1_, ...), custom_call_target="tpu_custom_call" | custom-call | tf_op jit(solution)/shard_map/pallas_call | solution.py:421

commit v2 on v1

v2 whole, which is shorter than its diff:
```python
import functools

import jax
import jax.numpy as jnp
import numpy as np
from jax import lax
from jax.experimental import pallas as pl
from jax.experimental.pallas import tpu as pltpu
from jax.sharding import PartitionSpec as P

MESH = pl.DeviceIdType.MESH
LEVELS = 4
NX, NY, NZ = 48, 128, 8

lift_alpha = -1.586134342059924
lift_beta = -0.052980118572961
lift_gamma = 0.882911075530934
lift_delta = 0.443506852043971
scale_low = 0.869864451624781
scale_high = 1.149604398860241


def lift_halves(even, odd, up, down):
    one = odd + lift_alpha * (even + up(even))
    two = even + lift_beta * (down(one) + one)
    three = one + lift_gamma * (two + up(two))
    four = two + lift_delta * (down(three) + three)
    return four * scale_low, three * scale_high


def operators(extent):
    tiles = 9
    line = np.zeros((tiles * extent, extent))
    line[4 * extent : 5 * extent] = np.eye(extent)
    found = []
    for level in range(LEVELS):
        low, high = lift_halves(
            line[0::2], line[1::2], lambda a: np.roll(a, -1, 0), lambda a: np.roll(a, 1, 0)
        )
        count = extent >> (level + 1)
        start = 4 * count
        pair = []
        for band in (low, high):
            rows = {}
            for k in range(band.shape[0]):
                if np.any(band[k]):
                    rows[k - start] = band[k]
            pair.append(rows)
        found.append(pair)
        line = low
    return found


ROWS_X = operators(NX)
ROWS_Y = operators(NY)
GROUPS = 4


def split_rows(pair, count):
    groups = {"own": [], "left": [], "right": [], "far": []}
    for band, rows in enumerate(pair):
        for k in sorted(rows):
            if k < -count or k >= 2 * count + 1:
                raise ValueError
            name = "left" if k < 0 else "own" if k < count else "right" if k < 2 * count else "far"
            groups[name].append((band, k, rows[k]))
    return groups


GX = [split_rows(ROWS_X[i], NX >> (i + 1)) for i in range(LEVELS)]
GY = [split_rows(ROWS_Y[i], NY >> (i + 1)) for i in range(LEVELS)]


def depth(level):
    return 8 >> level


def band_rows(level):
    count = (NX >> (level + 1)) * (1 if level == 0 else depth(level))
    return -(-count // 8) * 8


def x_own(level):
    n = 1 if level == 0 else depth(level)
    m = np.zeros((2 * band_rows(level), n * NX), np.float32)
    for band, k, w in GX[level]["own"]:
        for z in range(n):
            m[band * band_rows(level) + k * n + z, z * NX : (z + 1) * NX] = w
    return m


def edge_base(level, side):
    return band_rows(level) - EDGE_SPAN[level] if side == 0 else 0


def x_edge(level):
    if level == 0:
        m = np.zeros((16, 2 * NX), np.float32)
        for side, name in enumerate(("left", "right")):
            for i, (_, _, w) in enumerate(GX[0][name]):
                for v in range(2):
                    m[8 * side + 4 * v + i, v * NX : (v + 1) * NX] = w
        return m
    n, span, count = depth(level), EDGE_SPAN[level], NX >> (level + 1)
    far = GX[level]["far"]
    m = np.zeros((4 * span + (8 if far else 0), n * NX), np.float32)
    for side, name in enumerate(("left", "right")):
        for band, k, w in GX[level][name]:
            for z in range(n):
                to = (k + count if side == 0 else k - count) * n + z - edge_base(level, side)
                assert 0 <= to < span
                m[(2 * side + band) * span + to, z * NX : (z + 1) * NX] = w
    for band, k, w in far:
        assert band == 0 and k == 2 * count and n == 1
        m[4 * span] = w
    return m


def y_own(level):
    m = np.zeros((NY, 128), np.float32)
    for band, k, w in GY[level]["own"]:
        m[:, band * (NY >> (level + 1)) + k] = w
    return m


def y_edge(level):
    m = np.zeros((16, NY), np.float32)
    for side, name in enumerate(("left", "right")):
        for i, (_, _, w) in enumerate(GY[level][name]):
            m[8 * side + i] = w
    return m


def y_place(level):
    count = NY >> (level + 1)
    m = np.zeros((16, 128), np.float32)
    for side, name in enumerate(("left", "right")):
        for i, (band, k, _) in enumerate(GY[level][name]):
            m[8 * side + i, band * count + (k + count if side == 0 else k - count)] = 1
    return m


assert not any(GY[i]["far"] for i in range(LEVELS))

EDGE_SPAN = (8, 16, 16, 8)


def bf16_parts(m):
    parts, rest = [], m.astype(np.float32)
    for _ in range(3):
        part = rest.astype(jnp.bfloat16)
        parts.append(part)
        rest = rest - part.astype(np.float32)
    return parts


def packed_table(names, width):
    makers = {"x_own": x_own, "x_edge": x_edge, "y_own": y_own, "y_edge": y_edge, "y_place": y_place}
    parts, where, at = [], {}, 0
    for name, level in names:
        m = makers[name](level)
        wide = np.zeros((-(-m.shape[0] // 16) * 16, width), np.float32)
        wide[: m.shape[0], : m.shape[1]] = m
        if name == "y_place":
            stacked_parts = [wide.astype(jnp.bfloat16)] * 3
        else:
            stacked_parts = bf16_parts(wide)
        parts.extend(stacked_parts)
        where[name, level] = (at, wide.shape[0], m.shape[1])
        at += 3 * wide.shape[0]
    return np.concatenate(parts), where


ALL = [(name, i) for name in ("x_own", "x_edge", "y_own", "y_edge", "y_place") for i in range(LEVELS)]
BROAD = [("x_own", 1), ("x_edge", 1)]
TABLE, WHERE = packed_table([n for n in ALL if n not in BROAD], 128)
TABLE_B, WHERE_B = packed_table(BROAD, 256)

EDGE_AT = (0, 128, 192, 224)
EDGE_ROWS = (128, 64, 32, 16)
FAR_AT, EDGE_ALL = 240, 248
EDGE_TURN = (128, 64, 32, 16)
CORNER_AT = (0, 128, 256, 384)
CORNER_ROWS = (128, 128, 128, 64)
CORNER_FAR, CORNER_ALL = 448, 512
OWN_AT = (0, 768, 1152, 1280)
OWN_ROWS = (1536,) + tuple(2 * GROUPS * band_rows(i) for i in range(1, LEVELS))
OWN_ALL = 1408


def split(a):
    high = a.astype(jnp.bfloat16)
    rest = a - high.astype(jnp.float32)
    middle = rest.astype(jnp.bfloat16)
    return high, middle, (rest - middle.astype(jnp.float32)).astype(jnp.bfloat16)


def dot(a, b, contract=((1,), (0,))):
    return lax.dot_general(a, b, (contract, ((), ())), preferred_element_type=jnp.float32)


def dot_x(operator, parts):
    n = operator.shape[0] // 3
    one, two, last = dot(operator, parts[0]), dot(operator[: 2 * n], parts[1]), dot(operator[:n], parts[2])
    return one[:n] + ((one[n : 2 * n] + two[:n]) + (one[2 * n :] + two[n:] + last))


def dot_y(rows, operator):
    high, middle, low = rows
    n = operator.shape[0] // 3
    o_high, o_middle = operator[:n], operator[n : 2 * n]
    one = dot(jnp.concatenate([high, middle], 1), jnp.concatenate([o_high, o_high], 0))
    two = dot(jnp.concatenate([low, high], 1), operator[: 2 * n])
    last = dot(jnp.concatenate([middle, high], 1), operator[n:])
    return one + (two + last)


def dot_edge(operator, rows):
    n = operator.shape[0] // 3
    contract = ((1,), (1,))
    one, two, last = dot(operator, rows[0], contract), dot(operator[: 2 * n], rows[1], contract), dot(operator[:n], rows[2], contract)
    return one[:n] + ((one[n : 2 * n] + two[:n]) + (one[2 * n :] + two[n:] + last))


def place(c, operator):
    return dot(jnp.concatenate(split(c), 0), operator, ((0,), (0,)))


def stacked(wide, planes):
    return jnp.concatenate([wide[:, 128 * p : 128 * (p + 1)] for p in range(planes)], axis=0)


def planes_kernel(fields, table_in, broad_in, table, broad, wide1, wide2, wide3, wide4, raw, send, recv, local):
    wides = (wide1, wide2, wide3, wide4)
    gx, gy, gz = lax.axis_index("gx"), lax.axis_index("gy"), lax.axis_index("gz")
    partner = (gx, gy, 1 - gz)
    barrier = pltpu.get_barrier_semaphore()
    pl.semaphore_signal(barrier, inc=1, device_id=partner, device_id_type=MESH)
    keeps = [
        pltpu.make_async_copy(fields.at[2 * gz + v], raw.at[v, pl.ds(NZ * gz, NZ)], local.at[2 + v]) for v in range(2)
    ]
    for keep in keeps:
        keep.start()
    fill = pltpu.make_async_copy(table_in, table, local.at[0])
    fill.start()
    fill_b = pltpu.make_async_copy(broad_in, broad, local.at[1])
    fill_b.start()
    pl.semaphore_wait(barrier, 1)
    swaps = [
        pltpu.make_async_remote_copy(
            src_ref=fields.at[2 - 2 * gz + v], dst_ref=raw.at[v, pl.ds(NZ * gz, NZ)],
            send_sem=send.at[v], recv_sem=recv.at[v], device_id=partner, device_id_type=MESH,
        )
        for v in range(2)
    ]
    for swap in swaps:
        swap.start()
    for v in range(2):
        keeps[v].wait()
        swaps[v].wait_recv()
        planes = [raw[v, i] for i in range(2 * NZ)]
        for level in range(LEVELS):
            half = len(planes) // 2
            even, odd = planes[0::2], planes[1::2]
            one = [odd[k] + lift_alpha * (even[k] + even[(k + 1) % half]) for k in range(half)]
            two = [even[k] + lift_beta * (one[k - 1] + one[k]) for k in range(half)]
            three = [one[k] + lift_gamma * (two[k] + two[(k + 1) % half]) for k in range(half)]
            four = [two[k] + lift_delta * (three[k - 1] + three[k]) for k in range(half)]
            low = [a * scale_low for a in four]
            high = [a * scale_high for a in three]
            for i, plane in enumerate(low + high):
                for j, part in enumerate(split(plane)):
                    if level == 0:
                        wide1[j, NX * v : NX * (v + 1), 128 * i : 128 * (i + 1)] = part
                    else:
                        g, z = 2 * v + i // half, i % half
                        wides[level][j, NX * z : NX * (z + 1), 128 * g : 128 * (g + 1)] = part
            planes = low
    fill.wait()
    fill_b.wait()
    for swap in swaps:
        swap.wait_send()


def kernel(ring_x, ring_y, *refs):
    table, broad = refs[:2]
    wides = refs[2:6]
    outs = refs[6:11]
    (v2, v3, v4, m_out, c_out, k_out, m_in, c_in, k_in, far_m, far_k, send, recv) = refs[11:]
    values = (None, v2, v3, v4)

    def op(name, level):
        if (name, level) in WHERE_B:
            first, rows, columns = WHERE_B[name, level]
            return broad[first : first + 3 * rows, :columns]
        first, rows, columns = WHERE[name, level]
        return table[first : first + 3 * rows, :columns]

    gx, gy, gz = lax.axis_index("gx"), lax.axis_index("gy"), lax.axis_index("gz")

    def at(dx, dy):
        return (lax.rem(gx + dx + ring_x, ring_x), lax.rem(gy + dy + ring_y, ring_y), gz)

    near = [(dx, dy) for dx in (-1, 0, 1) for dy in (-1, 0, 1) if dx or dy]
    barrier = pltpu.get_barrier_semaphore()
    for d in near + [(-2, -1), (-2, 0), (-2, 1)]:
        pl.semaphore_signal(barrier, inc=1, device_id=at(*d), device_id_type=MESH)

    def copy(src, dst, slot, device):
        c = pltpu.make_async_remote_copy(
            src_ref=src, dst_ref=dst, send_sem=send.at[slot], recv_sem=recv.at[slot],
            device_id=device, device_id_type=MESH,
        )
        c.start()
        return c

    copies = []
    for level in range(LEVELS):
        edge = dot_x(op("x_edge", level), wides[level])
        lanes = 16 if level == 0 else GROUPS
        first, rows = EDGE_AT[level], EDGE_ROWS[level]
        corner_at, count = CORNER_AT[level], CORNER_ROWS[level]
        per = 8 if level == 0 else 2 * EDGE_SPAN[level]
        parts = [stacked(edge[:per], lanes), stacked(edge[per : 2 * per], lanes)]
        if level == 3:
            parts.append(stacked(edge[2 * per : 2 * per + 8], lanes))
        both = jnp.concatenate(parts, axis=0)
        both = split(both)
        done = dot_y(both, op("y_own", level))
        corner = dot_edge(op("y_edge", level), both)

        def closed(block):
            n = block.shape[0] * rows // count
            packed = block[:n]
            for g in range(1, count // rows):
                packed = packed + pltpu.roll(block[n * g : n * (g + 1)], EDGE_TURN[level] * g, 1)
            return packed

        for side in range(2):
            m_out[side, first : first + rows, :] = closed(done[count * side : count * (side + 1)])
            k_out[side, :, :, corner_at : corner_at + count] = corner[:, count * side : count * (side + 1)].reshape(2, 8, count)
        if level == 3:
            m_out[1, FAR_AT:EDGE_ALL, :] = closed(done[2 * count :])
            k_out[1, :, :, CORNER_FAR : CORNER_FAR + 32] = corner[:, 2 * count :].reshape(2, 8, 32)
    pl.semaphore_wait(barrier, 11)
    for side, dx in ((0, -1), (1, 1)):
        for up, dy in ((0, -1), (1, 1)):
            copies.append(copy(k_out.at[side, up], k_in.at[side, up], 2 + 2 * side + up, at(dx, dy)))
    for up, dy in ((0, -1), (1, 1)):
        copies.append(copy(k_out.at[1, up, :, pl.ds(384, 128)], far_k.at[up], 6 + up, at(2, dy)))
    copies.append(copy(m_out.at[1, pl.ds(FAR_AT, 8)], far_m, 8, at(2, 0)))
    for side, dx in ((0, -1), (1, 1)):
        copies.append(copy(m_out.at[side, pl.ds(0, FAR_AT)], m_in.at[side, pl.ds(0, FAR_AT)], side, at(dx, 0)))

    tall = []
    for level in range(LEVELS):
        if level == 0:
            pieces = [dot_x(op("x_own", 0), wides[0].at[:, NX * v : NX * (v + 1), :]) for v in range(2)]
            rows = jnp.concatenate([stacked(p[24 * bx : 24 * (bx + 1)], 16) for bx in range(2) for p in pieces], axis=0)
        else:
            rows = stacked(dot_x(op("x_own", level), wides[level]), GROUPS)
        first, count = OWN_AT[level], OWN_ROWS[level]
        rows = split(rows)
        c = dot_edge(op("y_edge", level), rows)
        if level == 0:
            count = count // 2
            c = c[:, :count].reshape(2, 8, count) + pltpu.roll(c[:, count:].reshape(2, 8, count), 4, 1)
        c_out[:, :, first : first + count] = c.reshape(2, 8, count)
        tall.append(rows)
    y_copies = [copy(c_out.at[up], c_in.at[up], 9 + up, at(0, dy)) for up, dy in ((0, -1), (1, 1))]

    def level_one(full, add):
        for bx in range(2):
            for v in range(2):
                for bz in range(2):
                    start = ((bx * 2 + v) * 2 + bz) * 192
                    for by in range(2):
                        b = 4 * bz + 2 * by + bx
                        if b:
                            block = full[by][start : start + 192, :64].reshape(8, 24, 64)
                            if add:
                                outs[0][b - 1, v] += block
                            else:
                                outs[0][b - 1, v] = block

    full = dot_y(tall[0], op("y_own", 0))
    level_one((full, pltpu.roll(full, 64, 1)), False)
    for level in range(1, LEVELS):
        values[level][...] = dot_y(tall[level], op("y_own", level)).reshape(GROUPS, 2, band_rows(level), 128)

    for c in y_copies:
        c.wait()
    for level in range(LEVELS):
        first, count = OWN_AT[level], OWN_ROWS[level]
        if level == 0:
            c = c_in[:, :, first : first + count // 2]
            c = jnp.concatenate([c, pltpu.roll(c, 4, 1)], axis=2).reshape(16, count)
            full = place(c, op("y_place", 0))
            level_one((full, pltpu.roll(full, 64, 1)), True)
        else:
            c = c_in[:, :, first : first + count].reshape(16, count)
            values[level][...] += place(c, op("y_place", level)).reshape(GROUPS, 2, band_rows(level), 128)

    for c in copies:
        c.wait()
    row = lax.broadcasted_iota(jnp.int32, (1, 8, 128), 1)

    def shifted(block, start, count, to):
        turn = (to - start) % 8
        if turn:
            block = pltpu.roll(block, turn, 1)
        return jnp.where((row >= to) & (row < to + count), block, 0.0)

    for level in reversed(range(LEVELS)):
        first, rows = EDGE_AT[level], EDGE_ROWS[level]
        corner_at, count = CORNER_AT[level], CORNER_ROWS[level]

        def opened(packed):
            parts = [packed]
            for g in range(1, count // rows):
                parts.append(pltpu.roll(packed, 128 - EDGE_TURN[level] * g, 1))
            return jnp.concatenate(parts, axis=0)

        for side in range(2):
            k = k_in[side, :, :, corner_at : corner_at + count].reshape(16, count)
            m = opened(m_in[side, first : first + rows, :]) + place(k, op("y_place", level))
            if level:
                span, base = EDGE_SPAN[level], edge_base(level, side)
                values[level][:, :, base : base + span, :] += m.reshape(GROUPS, 2, span, 128)
                continue
            edges = GX[0]["right" if side else "left"]
            for by in range(2):
                block = (pltpu.roll(m, 64, 1) if by else m).reshape(16, 8, 128)
                for bx in range(2):
                    hits = [i for i, h in enumerate(edges) if h[0] == bx]
                    k0 = edges[hits[0]][1]
                    to = k0 - 24 if side else k0 + 24
                    base = to - to % 8
                    for v in range(2):
                        add = shifted(block, hits[0] + 4 * v, len(hits), to - base)[:, :, :64]
                        for bz in range(2):
                            b = 4 * bz + 2 * by + bx
                            if b:
                                outs[0][b - 1, v, :, base : base + 8, :] += add[8 * bz : 8 * bz + 8]
        if level == 3:
            k = far_k[:, :, 64:96].reshape(16, 32)
            far = opened(far_m[...]) + place(k, op("y_place", level))
            values[level][:, 0, 0:8, :] += far.reshape(GROUPS, 8, 128)
        if level:
            n, xs, columns = depth(level), NX >> (level + 1), NY >> (level + 1)
            for v in range(2):
                for bz in range(2):
                    for bx in range(2):
                        got = values[level][2 * v + bz, bx, : xs * n, :]
                        for by in range(2):
                            b = 4 * bz + 2 * by + bx
                            part = got[:, columns * by : columns * (by + 1)].reshape(xs, n, columns)
                            if b:
                                outs[level][b - 1, v] = part
                            elif level == 3:
                                outs[4][xs * v : xs * (v + 1)] = part


def finish(*refs):
    ins, outs, sems = refs[:5], refs[5:10], refs[10]
    copies = [pltpu.make_async_copy(ins[i], outs[i], sems.at[i]) for i in range(5)]
    for c in copies:
        c.start()
    for c in copies:
        c.wait()


def in_hbm(array):
    return pltpu.with_memory_space_constraint(array, pltpu.HBM)


def in_vmem(array):
    return pltpu.with_memory_space_constraint(array, pltpu.VMEM)


def solution(mesh):
    ring_x, ring_y = mesh.shape["gx"], mesh.shape["gy"]
    shapes = [(7, 2, 8, NX >> 1, NY >> 1)]
    shapes += [(7, 2, NX >> (i + 1), 8 >> i, NY >> (i + 1)) for i in range(1, LEVELS)]
    shapes.append((2 * (NX >> LEVELS), 1, NY >> LEVELS))
    f32 = jnp.float32
    wide_shapes = [(3, 2 * NX, 16 * NY)] + [(3, depth(i) * NX, GROUPS * NY) for i in range(1, LEVELS)]
    any_ = pl.BlockSpec(memory_space=pl.ANY)
    vmem = pl.BlockSpec(memory_space=pltpu.VMEM)

    def body(fields):
        prepared = pl.pallas_call(
            planes_kernel,
            out_shape=[pltpu.VMEM(s, jnp.bfloat16) for s in [TABLE.shape, TABLE_B.shape] + wide_shapes],
            in_specs=[any_] * 3,
            out_specs=[vmem] * 6,
            scratch_shapes=[
                pltpu.VMEM((2, 2 * NZ, NX, NY), f32),
                pltpu.SemaphoreType.DMA((2,)),
                pltpu.SemaphoreType.DMA((2,)),
                pltpu.SemaphoreType.DMA((4,)),
            ],
            compiler_params=pltpu.CompilerParams(
                collective_id=1, has_side_effects=True, vmem_limit_bytes=16 << 20
            ),
        )(in_hbm(fields), in_hbm(jnp.asarray(TABLE)), in_hbm(jnp.asarray(TABLE_B)))
        values = pl.pallas_call(
            functools.partial(kernel, ring_x, ring_y),
            out_shape=[pltpu.VMEM(s, f32) for s in shapes],
            in_specs=[vmem] * 6,
            out_specs=[vmem] * 5,
            scratch_shapes=[pltpu.VMEM((GROUPS, 2, band_rows(i), 128), f32) for i in range(1, LEVELS)]
            + [pltpu.VMEM(s, f32) for s in ((2, EDGE_ALL, 128), (2, 8, OWN_ALL), (2, 2, 8, CORNER_ALL))] * 2
            + [
                pltpu.VMEM((8, 128), f32),
                pltpu.VMEM((2, 8, 128), f32),
                pltpu.SemaphoreType.DMA((11,)),
                pltpu.SemaphoreType.DMA((11,)),
            ],
            compiler_params=pltpu.CompilerParams(
                collective_id=0, has_side_effects=True, vmem_limit_bytes=40 << 20
            ),
        )(*[in_vmem(a) for a in prepared])
        outs = pl.pallas_call(
            finish,
            out_shape=[pltpu.HBM(s, f32) for s in shapes],
            in_specs=[vmem] * 5,
            out_specs=[any_] * 5,
            scratch_shapes=[pltpu.SemaphoreType.DMA((5,))],
        )(*[in_vmem(a) for a in values])
        small = [jnp.swapaxes(o, 2, 3) for o in outs[1:4]]
        return (outs[0], *small, outs[4].reshape(2, 1, NX >> LEVELS, NY >> LEVELS))

    in_specs = (P(None, "gz", "gx", "gy"),)
    out_specs = tuple([P(None, "gz", None, "gx", "gy")] * 4 + [P("gz", None, "gx", "gy")])
    return jax.shard_map(body, mesh=mesh, in_specs=in_specs, out_specs=out_specs, check_vma=False)
```

time: 28.1 us -> 26.8 us (0.954)
  Pallas kernels: 27.3 us -> 26 us
    pallas_call x1, Pallas kernels: 2.05 us -> 1.25 us  [body(): pl.pallas_call(finish, out_shape=[pltpu.HBM(s, f32) for s in shapes], in_...]
    pallas_call x1, Pallas kernels: 15.7 us -> 15.1 us  [body(): pl.pallas_call(functools.partial(kernel, ring_x, ring_y), out_shape=[pltp...]
where the time goes in v2:
time: 26.8 us; the launch traced here: 26.6 us
  Pallas kernels  26 us (97%)
  between operations  0.65 us (2%)
    pallas_call x1, Pallas kernels, body(): pl.pallas_call(functools.partial(kernel, ring_x, ring_y), out_shape=[pltp...  15.1 us
    pallas_call x1, Pallas kernels, body(): pl.pallas_call(planes_kernel, out_shape=[pltpu.VMEM(s, jnp.bfloat16) for...  9.62 us
    pallas_call x1, Pallas kernels, body(): pl.pallas_call(finish, out_shape=[pltpu.HBM(s, f32) for s in shapes], in_...  1.25 us

profile of v2, /device:TPU:1, one launch (start us, length us, event | category | flops | bytes accessed | tf_op | source)
XLA Modules:
  0.0 26.6 jit_solution(13186925768619305689)
XLA Ops:
  0.6 9.6 %shard_map.74 = (bf16[2592,128]{1,0:T(8,128)(2,1)S(1)}, bf16[480,256]{1,0:T(8,128)(2,1)S(1)}, bf16[3,96,2048]{2,1,0:T(8,128)(2,1)S(1)}, bf16[3,192,512]{2,1,0:T(...) custom-call(f32[4,8,48,128]{3,2,1,0:T(8,128)} %fields.1, ...), custom_call_target="tpu_custom_call" | custom-call | tf_op jit(solution)/shard_map/pallas_call | solution.py:492
  10.3 15.1 %shard_map.75 = (f32[7,2,8,24,64]{4,3,2,1,0:T(8,128)S(1)}, f32[7,2,12,4,32]{4,3,2,1,0:T(4,128)S(1)}, f32[7,2,6,2,16]{4,3,2,1,0:T(2,128)S(1)}, f32[7,2,3,1,8]{4,3,2,1,0:T(1,128)S(1)}, f32[6,1,8]{2,1,0:T(1,128)S(1)}) custom-call(bf16[2592,128]{1,0:T(8,128)(2,1)S(1)} %get-tuple-element.21.refs_0_, bf16[480,256]{1,0:T(8,128)(2,1)S(1)} %get-tuple-element.22.refs_1_, ...), custom_call_target="tpu_custom_call" | custom-call | tf_op jit(solution)/shard_map/pallas_call | solution.py:507
  25.4 1.3 %shard_map.76 = (f32[7,2,8,24,64]{4,3,2,1,0:T(8,128)}, f32[7,2,12,4,32]{4,3,2,1,0:T(4,128)}, f32[7,2,6,2,16]{4,3,2,1,0:T(2,128)}, f32[7,2,3,1,8]{4,3,2,1,0:T(1,128)}, f32[6,1,8]{2,1,0:T(1,128)}) custom-call(f32[7,2,8,24,64]{4,3,2,1,0:T(8,128)S(1)} %get-tuple-element.27.refs_0_, f32[7,2,12,4,32]{4,3,2,1,0:T(4,128)S(1)} %get-tuple-element.28.refs_1_, ...), custom_call_target="tpu_custom_call" | custom-call | tf_op jit(solution)/shard_map/pallas_call | solution.py:524

commit v3 on v2

--- a/solution.py
+++ b/solution.py
@@ -154,14 +154,26 @@
     return parts
 
 
+def x_first(v):
+    m = np.concatenate([x_own(0), x_edge(0)[:, v * NX : (v + 1) * NX]])
+    high, middle, low = bf16_parts(m)
+    none = np.zeros_like(low)
+    return np.block([[high, high, high], [middle, middle, none], [low, none, none]])
+
+
+def lanes_on(m):
+    return np.roll(m, 64, 1)
+
+
 def packed_table(names, width):
-    makers = {"x_own": x_own, "x_edge": x_edge, "y_own": y_own, "y_edge": y_edge, "y_place": y_place}
+    makers = {"x_own": x_own, "x_edge": x_edge, "y_own": y_own, "y_edge": y_edge, "y_place": y_place,
+              "y_high": lambda i: lanes_on(y_own(i)), "y_place_high": lambda i: lanes_on(y_place(i))}
     parts, where, at = [], {}, 0
     for name, level in names:
         m = makers[name](level)
         wide = np.zeros((-(-m.shape[0] // 16) * 16, width), np.float32)
         wide[: m.shape[0], : m.shape[1]] = m
-        if name == "y_place":
+        if name.startswith("y_place"):
             stacked_parts = [wide.astype(jnp.bfloat16)] * 3
         else:
             stacked_parts = bf16_parts(wide)
@@ -173,8 +185,12 @@
 
 ALL = [(name, i) for name in ("x_own", "x_edge", "y_own", "y_edge", "y_place") for i in range(LEVELS)]
 BROAD = [("x_own", 1), ("x_edge", 1)]
-TABLE, WHERE = packed_table([n for n in ALL if n not in BROAD], 128)
+NARROW = [n for n in ALL if n not in BROAD + [("x_own", 0), ("x_edge", 0)]]
+TABLE, WHERE = packed_table(NARROW + [("y_high", 0), ("y_place_high", 0)], 128)
 TABLE_B, WHERE_B = packed_table(BROAD, 256)
+FIRST_AT = TABLE_B.shape[0]
+TABLE_B = np.concatenate([TABLE_B] + [np.pad(x_first(v), ((0, 0), (0, 256 - 3 * NX))) for v in range(2)])
+FIRST_ROWS = (TABLE_B.shape[0] - FIRST_AT) // 2
 
 EDGE_AT = (0, 128, 192, 224)
 EDGE_ROWS = (128, 64, 32, 16)
@@ -230,8 +246,7 @@
     return jnp.concatenate([wide[:, 128 * p : 128 * (p + 1)] for p in range(planes)], axis=0)
 
 
-def planes_kernel(fields, table_in, broad_in, table, broad, wide1, wide2, wide3, wide4, raw, send, recv, local):
-    wides = (wide1, wide2, wide3, wide4)
+def swap_kernel(fields, table_in, broad_in, table, broad, raw, send, recv, local):
     gx, gy, gz = lax.axis_index("gx"), lax.axis_index("gy"), lax.axis_index("gz")
     partner = (gx, gy, 1 - gz)
     barrier = pltpu.get_barrier_semaphore()
@@ -257,7 +272,44 @@
         swap.start()
     for v in range(2):
         keeps[v].wait()
-        swaps[v].wait_recv()
+        swaps[v].wait()
+    fill.wait()
+    fill_b.wait()
+
+
+def kernel(ring_x, ring_y, *refs):
+    table, broad, raw = refs[:3]
+    outs = refs[3:8]
+    (wide1, wide2, wide3, wide4, v2, v3, v4, m_out, c_out, k_out, m_in, c_in, k_in, far_m, far_k, send, recv) = refs[8:]
+    wides = (wide1, wide2, wide3, wide4)
+    values = (None, v2, v3, v4)
+
+    def op(name, level):
+        if (name, level) in WHERE_B:
+            first, rows, columns = WHERE_B[name, level]
+            return broad[first : first + 3 * rows, :columns]
+        first, rows, columns = WHERE[name, level]
+        return table[first : first + 3 * rows, :columns]
+
+    gx, gy, gz = lax.axis_index("gx"), lax.axis_index("gy"), lax.axis_index("gz")
+
+    def at(dx, dy):
+        return (lax.rem(gx + dx + ring_x, ring_x), lax.rem(gy + dy + ring_y, ring_y), gz)
+
+    near = [(dx, dy) for dx in (-1, 0, 1) for dy in (-1, 0, 1) if dx or dy]
+    barrier = pltpu.get_barrier_semaphore()
+    for d in near + [(-2, -1), (-2, 0), (-2, 1)]:
+        pl.semaphore_signal(barrier, inc=1, device_id=at(*d), device_id_type=MESH)
+
+    def copy(src, dst, slot, device):
+        c = pltpu.make_async_remote_copy(
+            src_ref=src, dst_ref=dst, send_sem=send.at[slot], recv_sem=recv.at[slot],
+            device_id=device, device_id_type=MESH,
+        )
+        c.start()
+        return c
+
+    for v in range(2):
         planes = [raw[v, i] for i in range(2 * NZ)]
         for level in range(LEVELS):
             half = len(planes) // 2
@@ -271,52 +323,21 @@
             for i, plane in enumerate(low + high):
                 for j, part in enumerate(split(plane)):
                     if level == 0:
-                        wide1[j, NX * v : NX * (v + 1), 128 * i : 128 * (i + 1)] = part
+                        wide1[v, NX * j : NX * (j + 1), 128 * i : 128 * (i + 1)] = part
                     else:
                         g, z = 2 * v + i // half, i % half
                         wides[level][j, NX * z : NX * (z + 1), 128 * g : 128 * (g + 1)] = part
             planes = low
-    fill.wait()
-    fill_b.wait()
-    for swap in swaps:
-        swap.wait_send()
-
-
-def kernel(ring_x, ring_y, *refs):
-    table, broad = refs[:2]
-    wides = refs[2:6]
-    outs = refs[6:11]
-    (v2, v3, v4, m_out, c_out, k_out, m_in, c_in, k_in, far_m, far_k, send, recv) = refs[11:]
-    values = (None, v2, v3, v4)
-
-    def op(name, level):
-        if (name, level) in WHERE_B:
-            first, rows, columns = WHERE_B[name, level]
-            return broad[first : first + 3 * rows, :columns]
-        first, rows, columns = WHERE[name, level]
-        return table[first : first + 3 * rows, :columns]
-
-    gx, gy, gz = lax.axis_index("gx"), lax.axis_index("gy"), lax.axis_index("gz")
-
-    def at(dx, dy):
-        return (lax.rem(gx + dx + ring_x, ring_x), lax.rem(gy + dy + ring_y, ring_y), gz)
-
-    near = [(dx, dy) for dx in (-1, 0, 1) for dy in (-1, 0, 1) if dx or dy]
-    barrier = pltpu.get_barrier_semaphore()
-    for d in near + [(-2, -1), (-2, 0), (-2, 1)]:
-        pl.semaphore_signal(barrier, inc=1, device_id=at(*d), device_id_type=MESH)
-
-    def copy(src, dst, slot, device):
-        c = pltpu.make_async_remote_copy(
-            src_ref=src, dst_ref=dst, send_sem=send.at[slot], recv_sem=recv.at[slot],
-            device_id=device, device_id_type=MESH,
-        )
-        c.start()
-        return c
 
     copies = []
+    first_own, first_edge = [], 0.0
+    for v in range(2):
+        done = dot(broad[FIRST_AT + FIRST_ROWS * v : FIRST_AT + FIRST_ROWS * (v + 1), : 3 * NX], wide1[v])
+        done = done[:64] + (done[64:128] + done[128:])
+        first_own.append(done[:NX])
+        first_edge = first_edge + done[NX:]
     for level in range(LEVELS):
-        edge = dot_x(op("x_edge", level), wides[level])
+        edge = first_edge if level == 0 else dot_x(op("x_edge", level), wides[level])
         lanes = 16 if level == 0 else GROUPS
         first, rows = EDGE_AT[level], EDGE_ROWS[level]
         corner_at, count = CORNER_AT[level], CORNER_ROWS[level]
@@ -355,8 +376,7 @@
     tall = []
     for level in range(LEVELS):
         if level == 0:
-            pieces = [dot_x(op("x_own", 0), wides[0].at[:, NX * v : NX * (v + 1), :]) for v in range(2)]
-            rows = jnp.concatenate([stacked(p[24 * bx : 24 * (bx + 1)], 16) for bx in range(2) for p in pieces], axis=0)
+            rows = jnp.concatenate([stacked(p[24 * bx : 24 * (bx + 1)], 16) for bx in range(2) for p in first_own], axis=0)
         else:
             rows = stacked(dot_x(op("x_own", level), wides[level]), GROUPS)
         first, count = OWN_AT[level], OWN_ROWS[level]
@@ -377,14 +397,13 @@
                     for by in range(2):
                         b = 4 * bz + 2 * by + bx
                         if b:
-                            block = full[by][start : start + 192, :64].reshape(8, 24, 64)
+                            block = full[start : start + 192, 128 * by : 128 * by + 64].reshape(8, 24, 64)
                             if add:
                                 outs[0][b - 1, v] += block
                             else:
                                 outs[0][b - 1, v] = block
 
-    full = dot_y(tall[0], op("y_own", 0))
-    level_one((full, pltpu.roll(full, 64, 1)), False)
+    level_one(dot_y(tall[0], jnp.concatenate([op("y_own", 0), op("y_high", 0)], 1)), False)
     for level in range(1, LEVELS):
         values[level][...] = dot_y(tall[level], op("y_own", level)).reshape(GROUPS, 2, band_rows(level), 128)
 
@@ -395,8 +414,7 @@
         if level == 0:
             c = c_in[:, :, first : first + count // 2]
             c = jnp.concatenate([c, pltpu.roll(c, 4, 1)], axis=2).reshape(16, count)
-            full = place(c, op("y_place", 0))
-            level_one((full, pltpu.roll(full, 64, 1)), True)
+            level_one(place(c, jnp.concatenate([op("y_place", 0), op("y_place_high", 0)], 1)), True)
         else:
             c = c_in[:, :, first : first + count].reshape(16, count)
             values[level][...] += place(c, op("y_place", level)).reshape(GROUPS, 2, band_rows(level), 128)
@@ -484,18 +502,18 @@
     shapes += [(7, 2, NX >> (i + 1), 8 >> i, NY >> (i + 1)) for i in range(1, LEVELS)]
     shapes.append((2 * (NX >> LEVELS), 1, NY >> LEVELS))
     f32 = jnp.float32
-    wide_shapes = [(3, 2 * NX, 16 * NY)] + [(3, depth(i) * NX, GROUPS * NY) for i in range(1, LEVELS)]
+    wide_shapes = [(2, 3 * NX, 16 * NY)] + [(3, depth(i) * NX, GROUPS * NY) for i in range(1, LEVELS)]
     any_ = pl.BlockSpec(memory_space=pl.ANY)
     vmem = pl.BlockSpec(memory_space=pltpu.VMEM)
 
     def body(fields):
         prepared = pl.pallas_call(
-            planes_kernel,
-            out_shape=[pltpu.VMEM(s, jnp.bfloat16) for s in [TABLE.shape, TABLE_B.shape] + wide_shapes],
+            swap_kernel,
+            out_shape=[pltpu.VMEM(t.shape, jnp.bfloat16) for t in (TABLE, TABLE_B)]
+            + [pltpu.VMEM((2, 2 * NZ, NX, NY), f32)],
             in_specs=[any_] * 3,
-            out_specs=[vmem] * 6,
+            out_specs=[vmem] * 3,
             scratch_shapes=[
-                pltpu.VMEM((2, 2 * NZ, NX, NY), f32),
                 pltpu.SemaphoreType.DMA((2,)),
                 pltpu.SemaphoreType.DMA((2,)),
                 pltpu.SemaphoreType.DMA((4,)),
@@ -507,9 +525,10 @@
         values = pl.pallas_call(
             functools.partial(kernel, ring_x, ring_y),
             out_shape=[pltpu.VMEM(s, f32) for s in shapes],
-            in_specs=[vmem] * 6,
+            in_specs=[vmem] * 3,
             out_specs=[vmem] * 5,
-            scratch_shapes=[pltpu.VMEM((GROUPS, 2, band_rows(i), 128), f32) for i in range(1, LEVELS)]
+            scratch_shapes=[pltpu.VMEM(s, jnp.bfloat16) for s in wide_shapes]
+            + [pltpu.VMEM((GROUPS, 2, band_rows(i), 128), f32) for i in range(1, LEVELS)]
             + [pltpu.VMEM(s, f32) for s in ((2, EDGE_ALL, 128), (2, 8, OWN_ALL), (2, 2, 8, CORNER_ALL))] * 2
             + [
                 pltpu.VMEM((8, 128), f32),

time: 26.8 us -> 26.3 us (0.981)
  Pallas kernels: 26 us -> 25.5 us
    pallas_call x1, Pallas kernels: 9.62 us -> 9.22 us  [body(): pl.pallas_call(swap_kernel, out_shape=[pltpu.VMEM(t.shape, jnp.bfloat16)...]
where the time goes in v3:
time: 26.3 us; the launch traced here: 26.2 us
  Pallas kernels  25.5 us (97%)
  between operations  0.65 us (2%)
    pallas_call x1, Pallas kernels, body(): pl.pallas_call(functools.partial(kernel, ring_x, ring_y), out_shape=[pltp...  15 us
    pallas_call x1, Pallas kernels, body(): pl.pallas_call(swap_kernel, out_shape=[pltpu.VMEM(t.shape, jnp.bfloat16)...  9.22 us
    pallas_call x1, Pallas kernels, body(): pl.pallas_call(finish, out_shape=[pltpu.HBM(s, f32) for s in shapes], in_...  1.25 us

profile of v3, /device:TPU:1, one launch (start us, length us, event | category | flops | bytes accessed | tf_op | source)
XLA Modules:
  0.0 26.2 jit_solution(13088769776913931182)
XLA Ops:
  0.6 9.2 %shard_map.74 = (bf16[2832,128]{1,0:T(8,128)(2,1)S(1)}, bf16[864,256]{1,0:T(8,128)(2,1)S(1)}, f32[2,16,48,128]{3,2,1,0:T(8,128)S(1)}) custom-call(f32[4,8,48,128]{3,2,1,0:T(8,128)} %fields.1, bf16[2832,128]{1,0:T(8,128)(2,1)} %constant.4.clone.table_in, bf16[864,256]{1,0:T(8,128)(2,1)} %constant.5.clone.broad_in), custom_call_target="tpu_custom_call" | custom-call | tf_op jit(solution)/shard_map/pallas_call | solution.py:510
  9.9 15.0 %shard_map.75 = (f32[7,2,8,24,64]{4,3,2,1,0:T(8,128)S(1)}, f32[7,2,12,4,32]{4,3,2,1,0:T(4,128)S(1)}, f32[7,2,6,2,16]{4,3,2,1,0:T(2,128)S(1)}, f32[7,2,3,1,8]{4,3,2,1,0:T(1,128)S(1)}, f32[6,1,8]{2,1,0:T(1,128)S(1)}) custom-call(bf16[2832,128]{1,0:T(8,128)(2,1)S(1)} %get-tuple-element.18.refs_0_, bf16[864,256]{1,0:T(8,128)(2,1)S(1)} %get-tuple-element.19.refs_1_, ...), custom_call_target="tpu_custom_call" | custom-call | tf_op jit(solution)/shard_map/pallas_call | solution.py:525
  24.9 1.3 %shard_map.76 = (f32[7,2,8,24,64]{4,3,2,1,0:T(8,128)}, f32[7,2,12,4,32]{4,3,2,1,0:T(4,128)}, f32[7,2,6,2,16]{4,3,2,1,0:T(2,128)}, f32[7,2,3,1,8]{4,3,2,1,0:T(1,128)}, f32[6,1,8]{2,1,0:T(1,128)}) custom-call(f32[7,2,8,24,64]{4,3,2,1,0:T(8,128)S(1)} %get-tuple-element.21.refs_0_, f32[7,2,12,4,32]{4,3,2,1,0:T(4,128)S(1)} %get-tuple-element.22.refs_1_, ...), custom_call_target="tpu_custom_call" | custom-call | tf_op jit(solution)/shard_map/pallas_call | solution.py:543

commit v4 on v3

--- a/solution.py
+++ b/solution.py
@@ -280,7 +280,9 @@
 def kernel(ring_x, ring_y, *refs):
     table, broad, raw = refs[:3]
     outs = refs[3:8]
-    (wide1, wide2, wide3, wide4, v2, v3, v4, m_out, c_out, k_out, m_in, c_in, k_in, far_m, far_k, send, recv) = refs[8:]
+    talls = refs[12:16]
+    (wide1, wide2, wide3, wide4) = refs[8:12]
+    (v2, v3, v4, m_out, c_out, k_out, m_in, c_in, k_in, far_m, far_k, send, recv) = refs[16:]
     wides = (wide1, wide2, wide3, wide4)
     values = (None, v2, v3, v4)
 
@@ -363,6 +365,24 @@
         if level == 3:
             m_out[1, FAR_AT:EDGE_ALL, :] = closed(done[2 * count :])
             k_out[1, :, :, CORNER_FAR : CORNER_FAR + 32] = corner[:, 2 * count :].reshape(2, 8, 32)
+    def own_x():
+        for level in range(LEVELS):
+            if level == 0:
+                rows = jnp.concatenate([stacked(p[24 * bx : 24 * (bx + 1)], 16) for bx in range(2) for p in first_own], axis=0)
+            else:
+                rows = stacked(dot_x(op("x_own", level), wides[level]), GROUPS)
+            first, count = OWN_AT[level], OWN_ROWS[level]
+            rows = split(rows)
+            c = dot_edge(op("y_edge", level), rows)
+            if level == 0:
+                count = count // 2
+                c = c[:, :count].reshape(2, 8, count) + pltpu.roll(c[:, count:].reshape(2, 8, count), 4, 1)
+            c_out[:, :, first : first + count] = c.reshape(2, 8, count)
+            for i in range(3):
+                talls[level][i] = rows[i]
+
+    ahead = jnp.logical_or(gx == 0, gy == 0)
+    pl.when(ahead)(own_x)
     pl.semaphore_wait(barrier, 11)
     for side, dx in ((0, -1), (1, 1)):
         for up, dy in ((0, -1), (1, 1)):
@@ -373,20 +393,7 @@
     for side, dx in ((0, -1), (1, 1)):
         copies.append(copy(m_out.at[side, pl.ds(0, FAR_AT)], m_in.at[side, pl.ds(0, FAR_AT)], side, at(dx, 0)))
 
-    tall = []
-    for level in range(LEVELS):
-        if level == 0:
-            rows = jnp.concatenate([stacked(p[24 * bx : 24 * (bx + 1)], 16) for bx in range(2) for p in first_own], axis=0)
-        else:
-            rows = stacked(dot_x(op("x_own", level), wides[level]), GROUPS)
-        first, count = OWN_AT[level], OWN_ROWS[level]
-        rows = split(rows)
-        c = dot_edge(op("y_edge", level), rows)
-        if level == 0:
-            count = count // 2
-            c = c[:, :count].reshape(2, 8, count) + pltpu.roll(c[:, count:].reshape(2, 8, count), 4, 1)
-        c_out[:, :, first : first + count] = c.reshape(2, 8, count)
-        tall.append(rows)
+    pl.when(jnp.logical_not(ahead))(own_x)
     y_copies = [copy(c_out.at[up], c_in.at[up], 9 + up, at(0, dy)) for up, dy in ((0, -1), (1, 1))]
 
     def level_one(full, add):
@@ -403,9 +410,9 @@
                             else:
                                 outs[0][b - 1, v] = block
 
-    level_one(dot_y(tall[0], jnp.concatenate([op("y_own", 0), op("y_high", 0)], 1)), False)
+    level_one(dot_y([talls[0][i] for i in range(3)], jnp.concatenate([op("y_own", 0), op("y_high", 0)], 1)), False)
     for level in range(1, LEVELS):
-        values[level][...] = dot_y(tall[level], op("y_own", level)).reshape(GROUPS, 2, band_rows(level), 128)
+        values[level][...] = dot_y([talls[level][i] for i in range(3)], op("y_own", level)).reshape(GROUPS, 2, band_rows(level), 128)
 
     for c in y_copies:
         c.wait()
@@ -528,6 +535,7 @@
             in_specs=[vmem] * 3,
             out_specs=[vmem] * 5,
             scratch_shapes=[pltpu.VMEM(s, jnp.bfloat16) for s in wide_shapes]
+            + [pltpu.VMEM((3, n, 128), jnp.bfloat16) for n in OWN_ROWS]
             + [pltpu.VMEM((GROUPS, 2, band_rows(i), 128), f32) for i in range(1, LEVELS)]
             + [pltpu.VMEM(s, f32) for s in ((2, EDGE_ALL, 128), (2, 8, OWN_ALL), (2, 2, 8, CORNER_ALL))] * 2
             + [

time: 26.3 us -> 26.3 us (level)
  no operation moved by 1% of the time
where the time goes in v4:
time: 26.3 us; the launch traced here: 26.2 us
  Pallas kernels  25.5 us (97%)
  between operations  0.65 us (2%)
    pallas_call x1, Pallas kernels, body(): pl.pallas_call(functools.partial(kernel, ring_x, ring_y), out_shape=[pltp...  15 us
    pallas_call x1, Pallas kernels, body(): pl.pallas_call(swap_kernel, out_shape=[pltpu.VMEM(t.shape, jnp.bfloat16)...  9.22 us
    pallas_call x1, Pallas kernels, body(): pl.pallas_call(finish, out_shape=[pltpu.HBM(s, f32) for s in shapes], in_...  1.25 us

profile of v4, /device:TPU:1, one launch (start us, length us, event | category | flops | bytes accessed | tf_op | source)
XLA Modules:
  0.0 26.2 jit_solution(5385855116134459081)
XLA Ops:
  0.6 9.2 %shard_map.74 = (bf16[2832,128]{1,0:T(8,128)(2,1)S(1)}, bf16[864,256]{1,0:T(8,128)(2,1)S(1)}, f32[2,16,48,128]{3,2,1,0:T(8,128)S(1)}) custom-call(f32[4,8,48,128]{3,2,1,0:T(8,128)} %fields.1, bf16[2832,128]{1,0:T(8,128)(2,1)} %constant.4.clone.table_in, bf16[864,256]{1,0:T(8,128)(2,1)} %constant.5.clone.broad_in), custom_call_target="tpu_custom_call" | custom-call | tf_op jit(solution)/shard_map/pallas_call | solution.py:517
  9.9 15.0 %shard_map.75 = (f32[7,2,8,24,64]{4,3,2,1,0:T(8,128)S(1)}, f32[7,2,12,4,32]{4,3,2,1,0:T(4,128)S(1)}, f32[7,2,6,2,16]{4,3,2,1,0:T(2,128)S(1)}, f32[7,2,3,1,8]{4,3,2,1,0:T(1,128)S(1)}, f32[6,1,8]{2,1,0:T(1,128)S(1)}) custom-call(bf16[2832,128]{1,0:T(8,128)(2,1)S(1)} %get-tuple-element.18.refs_0_, bf16[864,256]{1,0:T(8,128)(2,1)S(1)} %get-tuple-element.19.refs_1_, ...), custom_call_target="tpu_custom_call" | custom-call | tf_op jit(solution)/shard_map/pallas_call | solution.py:532
  24.9 1.3 %shard_map.76 = (f32[7,2,8,24,64]{4,3,2,1,0:T(8,128)}, f32[7,2,12,4,32]{4,3,2,1,0:T(4,128)}, f32[7,2,6,2,16]{4,3,2,1,0:T(2,128)}, f32[7,2,3,1,8]{4,3,2,1,0:T(1,128)}, f32[6,1,8]{2,1,0:T(1,128)}) custom-call(f32[7,2,8,24,64]{4,3,2,1,0:T(8,128)S(1)} %get-tuple-element.21.refs_0_, f32[7,2,12,4,32]{4,3,2,1,0:T(4,128)S(1)} %get-tuple-element.22.refs_1_, ...), custom_call_target="tpu_custom_call" | custom-call | tf_op jit(solution)/shard_map/pallas_call | solution.py:551

commit v5 on v4

--- a/solution.py
+++ b/solution.py
@@ -332,7 +332,7 @@
             planes = low
 
     copies = []
-    first_own, first_edge = [], 0.0
+    first_own, first_edge, edge_rows = [], 0.0, []
     for v in range(2):
         done = dot(broad[FIRST_AT + FIRST_ROWS * v : FIRST_AT + FIRST_ROWS * (v + 1), : 3 * NX], wide1[v])
         done = done[:64] + (done[64:128] + done[128:])
@@ -341,7 +341,6 @@
     for level in range(LEVELS):
         edge = first_edge if level == 0 else dot_x(op("x_edge", level), wides[level])
         lanes = 16 if level == 0 else GROUPS
-        first, rows = EDGE_AT[level], EDGE_ROWS[level]
         corner_at, count = CORNER_AT[level], CORNER_ROWS[level]
         per = 8 if level == 0 else 2 * EDGE_SPAN[level]
         parts = [stacked(edge[:per], lanes), stacked(edge[per : 2 * per], lanes)]
@@ -349,22 +348,30 @@
             parts.append(stacked(edge[2 * per : 2 * per + 8], lanes))
         both = jnp.concatenate(parts, axis=0)
         both = split(both)
-        done = dot_y(both, op("y_own", level))
+        edge_rows.append(both)
         corner = dot_edge(op("y_edge", level), both)
-
-        def closed(block):
-            n = block.shape[0] * rows // count
-            packed = block[:n]
-            for g in range(1, count // rows):
-                packed = packed + pltpu.roll(block[n * g : n * (g + 1)], EDGE_TURN[level] * g, 1)
-            return packed
-
         for side in range(2):
-            m_out[side, first : first + rows, :] = closed(done[count * side : count * (side + 1)])
             k_out[side, :, :, corner_at : corner_at + count] = corner[:, count * side : count * (side + 1)].reshape(2, 8, count)
         if level == 3:
-            m_out[1, FAR_AT:EDGE_ALL, :] = closed(done[2 * count :])
             k_out[1, :, :, CORNER_FAR : CORNER_FAR + 32] = corner[:, 2 * count :].reshape(2, 8, 32)
+
+    def edges_y():
+        for level in range(LEVELS):
+            first, rows, count = EDGE_AT[level], EDGE_ROWS[level], CORNER_ROWS[level]
+            done = dot_y(edge_rows[level], op("y_own", level))
+
+            def closed(block):
+                n = block.shape[0] * rows // count
+                packed = block[:n]
+                for g in range(1, count // rows):
+                    packed = packed + pltpu.roll(block[n * g : n * (g + 1)], EDGE_TURN[level] * g, 1)
+                return packed
+
+            for side in range(2):
+                m_out[side, first : first + rows, :] = closed(done[count * side : count * (side + 1)])
+            if level == 3:
+                m_out[1, FAR_AT:EDGE_ALL, :] = closed(done[2 * count :])
+
     def own_x():
         for level in range(LEVELS):
             if level == 0:
@@ -382,13 +389,19 @@
                 talls[level][i] = rows[i]
 
     ahead = jnp.logical_or(gx == 0, gy == 0)
-    pl.when(ahead)(own_x)
+
+    @pl.when(ahead)
+    def _():
+        edges_y()
+        own_x()
+
     pl.semaphore_wait(barrier, 11)
     for side, dx in ((0, -1), (1, 1)):
         for up, dy in ((0, -1), (1, 1)):
             copies.append(copy(k_out.at[side, up], k_in.at[side, up], 2 + 2 * side + up, at(dx, dy)))
     for up, dy in ((0, -1), (1, 1)):
         copies.append(copy(k_out.at[1, up, :, pl.ds(384, 128)], far_k.at[up], 6 + up, at(2, dy)))
+    pl.when(jnp.logical_not(ahead))(edges_y)
     copies.append(copy(m_out.at[1, pl.ds(FAR_AT, 8)], far_m, 8, at(2, 0)))
     for side, dx in ((0, -1), (1, 1)):
         copies.append(copy(m_out.at[side, pl.ds(0, FAR_AT)], m_in.at[side, pl.ds(0, FAR_AT)], side, at(dx, 0)))

time: 26.3 us -> 26.3 us (level)
  no operation moved by 1% of the time
where the time goes in v5:
time: 26.3 us; the launch traced here: 26.2 us
  Pallas kernels  25.5 us (97%)
  between operations  0.65 us (2%)
    pallas_call x1, Pallas kernels, body(): pl.pallas_call(functools.partial(kernel, ring_x, ring_y), out_shape=[pltp...  15 us
    pallas_call x1, Pallas kernels, body(): pl.pallas_call(swap_kernel, out_shape=[pltpu.VMEM(t.shape, jnp.bfloat16)...  9.22 us
    pallas_call x1, Pallas kernels, body(): pl.pallas_call(finish, out_shape=[pltpu.HBM(s, f32) for s in shapes], in_...  1.25 us

profile of v5, /device:TPU:1, one launch (start us, length us, event | category | flops | bytes accessed | tf_op | source)
XLA Modules:
  0.0 26.2 jit_solution(13887830127078157080)
XLA Ops:
  0.6 9.2 %shard_map.74 = (bf16[2832,128]{1,0:T(8,128)(2,1)S(1)}, bf16[864,256]{1,0:T(8,128)(2,1)S(1)}, f32[2,16,48,128]{3,2,1,0:T(8,128)S(1)}) custom-call(f32[4,8,48,128]{3,2,1,0:T(8,128)} %fields.1, bf16[2832,128]{1,0:T(8,128)(2,1)} %constant.4.clone.table_in, bf16[864,256]{1,0:T(8,128)(2,1)} %constant.5.clone.broad_in), custom_call_target="tpu_custom_call" | custom-call | tf_op jit(solution)/shard_map/pallas_call | solution.py:530
  9.9 15.0 %shard_map.75 = (f32[7,2,8,24,64]{4,3,2,1,0:T(8,128)S(1)}, f32[7,2,12,4,32]{4,3,2,1,0:T(4,128)S(1)}, f32[7,2,6,2,16]{4,3,2,1,0:T(2,128)S(1)}, f32[7,2,3,1,8]{4,3,2,1,0:T(1,128)S(1)}, f32[6,1,8]{2,1,0:T(1,128)S(1)}) custom-call(bf16[2832,128]{1,0:T(8,128)(2,1)S(1)} %get-tuple-element.18.refs_0_, bf16[864,256]{1,0:T(8,128)(2,1)S(1)} %get-tuple-element.19.refs_1_, ...), custom_call_target="tpu_custom_call" | custom-call | tf_op jit(solution)/shard_map/pallas_call | solution.py:545
  24.9 1.3 %shard_map.76 = (f32[7,2,8,24,64]{4,3,2,1,0:T(8,128)}, f32[7,2,12,4,32]{4,3,2,1,0:T(4,128)}, f32[7,2,6,2,16]{4,3,2,1,0:T(2,128)}, f32[7,2,3,1,8]{4,3,2,1,0:T(1,128)}, f32[6,1,8]{2,1,0:T(1,128)}) custom-call(f32[7,2,8,24,64]{4,3,2,1,0:T(8,128)S(1)} %get-tuple-element.21.refs_0_, f32[7,2,12,4,32]{4,3,2,1,0:T(4,128)S(1)} %get-tuple-element.22.refs_1_, ...), custom_call_target="tpu_custom_call" | custom-call | tf_op jit(solution)/shard_map/pallas_call | solution.py:564
